TPU v7x, 32 devices: a whole 2x2x4 slice. The times are simulated.
32 devices in a mesh: expert: 8 (over z, x), slab: 4 (over y, core).
Axes of the slice: x: 2, y: 2, z: 4, core: 2. Of those that a mesh axis runs over, the one named last changes fastest.
Arguments:
- tokens: bfloat16 [8192, 768], P('expert', 'slab'), may hold values from -6 to 6
- gate: float32 [8192], P('expert'), may hold values from 0.2 to 1
- routes: int32 [8192, 1], P('expert'), may hold values from 0 to 31; in each aligned block of 1024 rows (0 to 1023, 1024 to 2047, ...) at most 64 rows name the same one
- grad_out: bfloat16 [8192, 768], P('expert', 'slab'), may hold values from -6 to 6
- w_in: bfloat16 [32, 768, 3072], P('expert', None, 'slab'), may hold values from -0.21875 to 0.21875
- w_out: bfloat16 [32, 3072, 768], P('expert', 'slab'), may hold values from -0.109375 to 0.109375
Outputs:
- mixed: bfloat16 [8192, 768], P('expert', 'slab')
- grad_in: bfloat16 [8192, 768], P('expert', 'slab')
- grad_w_in: bfloat16 [32, 768, 3072], P('expert', None, 'slab')
- grad_w_out: bfloat16 [32, 3072, 768], P('expert', 'slab')
Inputs may be any that keep to these rules, and one draw needn't show every extreme that they name: `routes`: in each aligned block of 1024 rows no expert is named by more than 64 rows, a bound that some block reaches.
All inputs are finite; a program needn't handle non-finite values.
Results may differ from a plain program's by a relative error of at most 0.0095.
Values may be sent and summed in bfloat16 or wider, within the bound.
A program may use at most 128 MiB of HBM per device.

v0:
```python
import jax
import jax.numpy as jnp
from jax import lax
from jax.sharding import PartitionSpec as P


def shards(tokens, gate, routes, grad_out, w_in, w_out):
    tok_rows = tokens.shape[0]
    groups = lax.axis_size("expert")
    local_experts = w_in.shape[0]
    all_experts = groups * local_experts
    capacity = 2 * tok_rows // all_experts
    expert_ids = routes[:, 0]
    onehot = (expert_ids[:, None] == jnp.arange(all_experts, dtype=jnp.int32)[None, :]).astype(
        jnp.int32
    )
    earlier = jnp.cumsum(onehot, axis=0) - onehot
    slot = jnp.sum(earlier * onehot, axis=1)
    target = expert_ids * capacity + slot
    placer = (
        jnp.arange(all_experts * capacity, dtype=jnp.int32)[:, None] == target[None, :]
    ).astype(jnp.bfloat16)

    def spread_rows(values):
        placed = jnp.dot(placer, values, preferred_element_type=jnp.float32).astype(jnp.bfloat16)
        return placed.reshape(all_experts, capacity, values.shape[1])

    def collect_rows(buffer):
        flat = buffer.reshape(all_experts * capacity, buffer.shape[2])
        return jnp.einsum("st,sd->td", placer, flat, preferred_element_type=jnp.float32)

    scaled = (gate[:, None] * grad_out.astype(jnp.float32)).astype(jnp.bfloat16)
    rows_send = spread_rows(tokens)
    grads_send = spread_rows(scaled)
    rows_recv = lax.all_to_all(rows_send, "expert", split_axis=0, concat_axis=1, tiled=True)
    rows_full = lax.all_gather(rows_recv, "slab", axis=2, tiled=True)
    pre = jnp.einsum("erd,edf->erf", rows_full, w_in, preferred_element_type=jnp.float32)
    hidden = jnp.maximum(pre, 0.0).astype(jnp.bfloat16)
    out_part = jnp.einsum("erf,efd->erd", hidden, w_out, preferred_element_type=jnp.float32).astype(
        jnp.bfloat16
    )
    out_sum = lax.psum_scatter(out_part, "slab", scatter_dimension=2, tiled=True).astype(
        jnp.float32
    )
    out_back = lax.all_to_all(
        out_sum.astype(jnp.bfloat16), "expert", split_axis=1, concat_axis=0, tiled=True
    )
    grads_recv = lax.all_to_all(grads_send, "expert", split_axis=0, concat_axis=1, tiled=True)
    grads_full = lax.all_gather(grads_recv, "slab", axis=2, tiled=True)
    grad_pre = jnp.einsum("erd,efd->erf", grads_full, w_out, preferred_element_type=jnp.float32)
    grad_hidden = jnp.where(pre > 0.0, grad_pre, 0.0).astype(jnp.bfloat16)
    grad_w_out = jnp.einsum(
        "erf,erd->efd", hidden, grads_full, preferred_element_type=jnp.float32
    ).astype(jnp.bfloat16)
    grad_w_in = jnp.einsum(
        "erd,erf->edf", rows_full, grad_hidden, preferred_element_type=jnp.float32
    ).astype(jnp.bfloat16)
    grad_part = jnp.einsum(
        "erf,edf->erd", grad_hidden, w_in, preferred_element_type=jnp.float32
    ).astype(jnp.bfloat16)
    grad_sum = lax.psum_scatter(grad_part, "slab", scatter_dimension=2, tiled=True).astype(
        jnp.float32
    )
    grad_back = lax.all_to_all(
        grad_sum.astype(jnp.bfloat16), "expert", split_axis=1, concat_axis=0, tiled=True
    )
    mixed = (gate[:, None] * collect_rows(out_back)).astype(jnp.bfloat16)
    grad_in = collect_rows(grad_back).astype(jnp.bfloat16)
    return (mixed, grad_in, grad_w_in, grad_w_out)


def solution(mesh):
    in_specs = (
        P("expert", "slab"),
        P("expert"),
        P("expert", None),
        P("expert", "slab"),
        P("expert", None, "slab"),
        P("expert", "slab", None),
    )
    out_specs = (
        P("expert", "slab"),
        P("expert", "slab"),
        P("expert", None, "slab"),
        P("expert", "slab", None),
    )
    return jax.shard_map(shards, mesh=mesh, in_specs=in_specs, out_specs=out_specs, check_vma=False)
```

profile of v0, /device:TPU:1, one launch (start us, length us, event | category | flops | bytes accessed | tf_op | source)
XLA Modules:
  0.0 239.2 jit_solution(7857763978922552648)
XLA Ops:
  7.2 0.7 fusion.18
  8.0 9.0 %reduce-window.6 = s32[32,8,128]{2,1,0:T(8,128)S(1)} reduce-window(s32[32,8,128]{2,1,0:T(8,128)S(1)} %fusion.18, s32[]{:T(128)} %constant.4.clone.1), window={size=1x1x128 pad=0_0x0_0x127_0}, to_apply=%region_0.0 | reduce-window | flops 4161536 | bytes 262148 | tf_op jit(solution)/shard_map/reduce-window
  17.4 0.7 fusion.17
  18.2 0.7 multiply_add_fusion
  18.9 1.9 fusion.8
  20.8 0.5 copy.30
  21.3 31.2 %all_to_all.66 = bf16[32,64,192]{2,1,0:T(8,128)(2,1)S(1)} all-to-all(bf16[32,64,192]{2,1,0:T(8,128)(2,1)S(1)} %bitcast.51), channel_id=1, replica_groups=mesh['expert'=8,'slab'=4] {'expert'}, dimensions={0} | all-to-all | bytes 1572864 | tf_op jit(solution)/shard_map/all_to_all | solution.py:35
  52.7 1.2 copy.32
  54.0 2.0 fusion.9
  56.0 0.5 copy.37
  56.5 28.8 %all_to_all.67 = bf16[32,64,192]{2,1,0:T(8,128)(2,1)S(1)} all-to-all(bf16[32,64,192]{2,1,0:T(8,128)(2,1)S(1)} %bitcast.53), channel_id=1, replica_groups=mesh['expert'=8,'slab'=4] {'expert'}, dimensions={0} | all-to-all | bytes 1572864 | tf_op jit(solution)/shard_map/all_to_all | solution.py:48
  85.4 1.2 copy.39
  86.8 6.4 %fusion.10 = (u8[512,768]{1,0:T(8,128)(4,1)S(1)}, bf16[4,512,768]{2,1,0:T(8,128)(2,1)S(1)}) fusion(bf16[4,512,768]{1,2,0:T(8,128)(2,1)} %all-gather.3.cloned.1.call-done, bf16[4,768,768]{2,1,0:T(8,128)(2,1)} %param.10), kind=kOutput, calls=%fused_computation.19 | convolution fusion | flops 2424963072 | bytes 11403264 | tf_op jit(solution)/shard_map/erd,edf->erf/dot_general | solution.py:37
  93.2 1.6 copy-done.4
  94.8 7.7 %convolution_convert_fusion.3 = bf16[4,512,768]{1,2,0:T(8,128)(2,1)} fusion(bf16[4,768,768]{2,1,0:T(8,128)(2,1)} %param.11, bf16[4,512,768]{2,1,0:T(8,128)(2,1)S(1)} %get-tuple-element.5), kind=kOutput, calls=%fused_computation.18 | convolution fusion | flops 2422210560 | bytes 11010048 | tf_op jit(solution)/shard_map/erf,efd->erd/dot_general | solution.py:39
  102.5 0.2 reduce-scatter.5.cloned.1.call-start
  102.8 13.2 %all-gather.5.cloned.1.call-done = bf16[4,512,768]{1,2,0:T(8,128)(2,1)} async-done(((bf16[4,512,192]{1,2,0:T(8,128)(2,1)}), bf16[4,512,768]{1,2,0:T(8,128)(2,1)}) %all-gather.5.cloned.1.call-update) | async-done | bytes 3145744 | tf_op jit(solution)/shard_map/all_gather | solution.py:49
  115.9 6.5 %select_convert_fusion = bf16[4,512,768]{2,1,0:T(8,128)(2,1)S(1)} fusion(bf16[4,512,768]{1,2,0:T(8,128)(2,1)} %all-gather.5.cloned.1.call-done, bf16[4,768,768]{2,1,0:T(8,128)(2,1)} %param.11, u8[512,768]{1,0:T(8,128)(4,1)S(1)} %get-tuple-element.4), kind=kOutput, calls=%fused_computation.7 | convolution fusion | flops 2425356288 | bytes 11403264 | tf_op jit(solution)/shard_map/erd,efd->erf/dot_general | solution.py:50
  122.4 1.7 copy-done.5
  124.1 4.0 %convolution_convert_fusion.2 = bf16[4,512,768]{1,2,0:T(8,128)(2,1)} fusion(bf16[4,512,768]{2,1,0:T(8,128)(2,1)S(1)} %select_convert_fusion, bf16[4,768,768]{2,1,0:T(8,128)(2,1)S(1)} %bitcast.67), kind=kOutput, calls=%fused_computation.17 | convolution fusion | flops 2417491968 | bytes 11010048 | tf_op jit(solution)/shard_map/erf,edf->erd/dot_general | solution.py:58
  128.1 28.5 %reduce-scatter.3.cloned.1.call-done = bf16[4,512,192]{1,2,0:T(8,128)(2,1)} async-done(((bf16[4,512,768]{1,2,0:T(8,128)(2,1)}), bf16[4,512,192]{1,2,0:T(8,128)(2,1)}) %reduce-scatter.3.cloned.1.call-update) | async-done | bytes 786448 | tf_op jit(solution)/shard_map/reduce_scatter | solution.py:42
  156.7 2.3 copy.34
  159.0 5.2 %all-to-all-start.1 = ((bf16[4,512,192]{2,0,1:T(4,128)(2,1)}), bf16[4,512,192]{2,0,1:T(4,128)(2,1)S(1)}, u32[]{:S(2)}, u32[]{:S(2)}) async-start(bf16[4,512,192]{2,0,1:T(4,128)(2,1)} %copy.34), calls=%async_computation.2 | async-start | bytes 2097152 | tf_op jit(solution)/shard_map/all_to_all | solution.py:45
  164.2 33.6 %reduce-scatter.5.cloned.1.call-done = bf16[4,512,192]{1,2,0:T(8,128)(2,1)} async-done(((bf16[4,512,768]{1,2,0:T(8,128)(2,1)}), bf16[4,512,192]{1,2,0:T(8,128)(2,1)}) %reduce-scatter.5.cloned.1.call-update) | async-done | bytes 786448 | tf_op jit(solution)/shard_map/reduce_scatter | solution.py:61
  197.8 2.4 copy.40
  200.1 5.2 %all-to-all-start.3 = ((bf16[4,512,192]{2,0,1:T(4,128)(2,1)}), bf16[4,512,192]{2,0,1:T(4,128)(2,1)S(1)}, u32[]{:S(2)}, u32[]{:S(2)}) async-start(bf16[4,512,192]{2,0,1:T(4,128)(2,1)} %copy.40), calls=%async_computation.5 | async-start | bytes 2097152 | tf_op jit(solution)/shard_map/all_to_all | solution.py:64
  205.4 8.1 %convolution_convert_fusion = bf16[4,768,768]{2,1,0:T(8,128)(2,1)} fusion(bf16[4,512,768]{1,2,0:T(8,128)(2,1)} %all-gather.5.cloned.1.call-done, bf16[4,512,768]{2,1,0:T(8,128)(2,1)} %copy-done.4), kind=kOutput, calls=%fused_computation.13 | convolution fusion | flops 2422996992 | bytes 11010048 | tf_op jit(solution)/shard_map/erf,erd->efd/dot_general | solution.py:52
  213.4 4.2 %convolution_convert_fusion.1 = bf16[4,768,768]{2,1,0:T(8,128)(2,1)} fusion(bf16[4,512,768]{1,2,0:T(8,128)(2,1)S(1)} %copy-done.1, bf16[4,512,768]{2,1,0:T(8,128)(2,1)S(1)} %copy-done.6), kind=kOutput, calls=%fused_computation.14 | convolution fusion | flops 2418278400 | bytes 11010048 | tf_op jit(solution)/shard_map/erd,erf->edf/dot_general | solution.py:55
  217.6 0.1 copy.35
  217.9 2.5 %fusion.12 = bf16[1024,192]{0,1:T(8,128)(2,1)} fusion(bf16[2048,192]{1,0:T(8,128)(2,1)S(1)} %bitcast.60, s32[1024]{0:T(1024)S(1)} %multiply_add_fusion, f32[1024]{0:T(1024)S(1)} %copy-done.3), kind=kOutput, calls=%fused_computation.21 | convolution fusion | flops 807796736 | bytes 1187840 | tf_op jit(solution)/shard_map/st,sd->td/dot_general | solution.py:30
  220.4 9.6 %all-to-all-done.3 = bf16[4,512,192]{2,0,1:T(4,128)(2,1)S(1)} async-done(((bf16[4,512,192]{2,0,1:T(4,128)(2,1)}), bf16[4,512,192]{2,0,1:T(4,128)(2,1)S(1)}, u32[]{:S(2)}, u32[]{:S(2)}) %all-to-all-start.3) | async-done | bytes 786464 | tf_op jit(solution)/shard_map/all_to_all | solution.py:64
  230.2 2.5 %fusion.13 = bf16[1024,192]{0,1:T(8,128)(2,1)} fusion(bf16[2048,192]{1,0:T(8,128)(2,1)S(1)} %bitcast.59, s32[1024]{0:T(1024)S(1)} %multiply_add_fusion), kind=kOutput, calls=%fused_computation.22 | convolution fusion | flops 807600128 | bytes 1183744 | tf_op jit(solution)/shard_map/st,sd->td/dot_general | solution.py:30
  (37 shorter events, 1.2 us)
Async XLA Ops:
  7.2 11.7 %copy-start = (bf16[1024,192]{0,1:T(8,128)(2,1)S(1)}, bf16[1024,192]{0,1:T(8,128)(2,1)}, u32[]{:S(2)}) copy-start(bf16[1024,192]{0,1:T(8,128)(2,1)} %param.6) | copy-start | bytes 1179652
  7.2 79.6 %all-gather.3.cloned.1.call-start = ((), (), s32[]{:S(2)}) async-start(), calls=%async_computation.6 | async-start | bytes 3932160 | tf_op jit(solution)/shard_map/all_gather | solution.py:36
  21.3 32.7 %copy-start.2 = (bf16[1024,192]{0,1:T(8,128)(2,1)S(1)}, bf16[1024,192]{0,1:T(8,128)(2,1)}, u32[]{:S(2)}) copy-start(bf16[1024,192]{0,1:T(8,128)(2,1)} %param.9) | copy-start | bytes 1179652
  21.3 32.7 %copy-start.3 = (f32[1024]{0:T(1024)S(1)}, f32[1024]{0:T(1024)}, u32[]{:S(2)}) copy-start(f32[1024]{0:T(1024)} %param.7) | copy-start | bytes 12292
  53.9 62.0 %all-gather.5.cloned.1.call-start = ((), (), s32[]{:S(2)}) async-start(), calls=%async_computation.8 | async-start | bytes 3932160 | tf_op jit(solution)/shard_map/all_gather | solution.py:49
  86.7 69.9 %reduce-scatter.3.cloned.1.call-start = ((), (), s32[]{:S(2)}) async-start(), calls=%async_computation.7 | async-start | bytes 3932160 | tf_op jit(solution)/shard_map/reduce_scatter | solution.py:42
  93.2 1.7 copy-start.4
  102.5 21.6 %slice-start = ((s8[4718592]{0:T(1024)(128)(4,1)}), s8[524288]{0:T(1024)(128)(4,1)S(1)}, s32[]{:S(2)}) async-start(s8[4718592]{0:T(1024)(128)(4,1)} %bitcast.66), calls=%async_computation.10 | async-start | bytes 1048576
  102.5 95.2 %reduce-scatter.5.cloned.1.call-start = ((), (), s32[]{:S(2)}) async-start(), calls=%async_computation.9 | async-start | bytes 3932160 | tf_op jit(solution)/shard_map/reduce_scatter | solution.py:61
  115.9 8.2 %slice-start.1 = ((s8[4718592]{0:T(1024)(128)(4,1)}), s8[4194304]{0:T(1024)(128)(4,1)S(1)}, s32[]{:S(2)}) async-start(s8[4718592]{0:T(1024)(128)(4,1)} %bitcast.66), calls=%async_computation.11 | async-start | bytes 8388608
  122.4 1.7 copy-start.5
  159.0 41.2 %all-to-all-start.1 = ((bf16[4,512,192]{2,0,1:T(4,128)(2,1)}), bf16[4,512,192]{2,0,1:T(4,128)(2,1)S(1)}, u32[]{:S(2)}, u32[]{:S(2)}) async-start(bf16[4,512,192]{2,0,1:T(4,128)(2,1)} %copy.34), calls=%async_computation.2 | async-start | bytes 2097152 | tf_op jit(solution)/shard_map/all_to_all | solution.py:45
  200.1 29.8 %all-to-all-start.3 = ((bf16[4,512,192]{2,0,1:T(4,128)(2,1)}), bf16[4,512,192]{2,0,1:T(4,128)(2,1)S(1)}, u32[]{:S(2)}, u32[]{:S(2)}) async-start(bf16[4,512,192]{2,0,1:T(4,128)(2,1)} %copy.40), calls=%async_computation.5 | async-start | bytes 2097152 | tf_op jit(solution)/shard_map/all_to_all | solution.py:64
  205.4 8.1 %copy-start.1 = (bf16[4,512,768]{1,2,0:T(8,128)(2,1)S(1)}, bf16[4,512,768]{1,2,0:T(8,128)(2,1)}, u32[]{:S(2)}) copy-start(bf16[4,512,768]{1,2,0:T(8,128)(2,1)} %all-gather.3.cloned.1.call-done) | copy-start | bytes 9437188
  205.4 8.1 %copy-start.6 = (bf16[4,512,768]{2,1,0:T(8,128)(2,1)S(1)}, bf16[4,512,768]{2,1,0:T(8,128)(2,1)}, u32[]{:S(2)}) copy-start(bf16[4,512,768]{2,1,0:T(8,128)(2,1)} %copy-done.5) | copy-start | bytes 9437188
Sparse Core Ops, SparseCore 0:
  54.0 29.0 all-gather.2
  86.8 29.0 all-gather.4
  119.0 37.5 reduce-scatter.2
  159.8 37.9 reduce-scatter.4
where the time goes:
time: 242 us; the launch traced here: 239 us
  waiting for transfers between devices  84.9 us (35%)
  blocking collectives  60 us (25%)
  matrix products  45.7 us (19%)
  between operations  14 us (6%)
  local copies, waits for them, and re-layouts  12.6 us (5%)
  other arithmetic  11.3 us (5%)
  starting transfers between devices  10.8 us (4%)
    reduce_scatter x1, waiting for transfers between devices, shards(): lax.psum_scatter(grad_part, 'slab', scatter_dimension=2, tiled=True)  33.6 us
    all_to_all x1, blocking collectives, shards(): lax.all_to_all(rows_send, 'expert', split_axis=0, concat_axis=1, tiled=True)  31.2 us
    all_to_all x1, blocking collectives, shards(): lax.all_to_all(grads_send, 'expert', split_axis=0, concat_axis=1, tiled=T...  28.8 us
    reduce_scatter x1, waiting for transfers between devices, shards(): lax.psum_scatter(out_part, 'slab', scatter_dimension=2, tiled=True)  28.5 us
    all_gather x1, waiting for transfers between devices, shards(): grads_full = lax.all_gather(grads_recv, 'slab', axis=2, tiled=True)  13.2 us
    all_to_all x1, waiting for transfers between devices, shards(): lax.all_to_all(grad_sum.astype(jnp.bfloat16), 'expert', split_axis=1, con...  9.57 us
    another operation x3, other arithmetic  9.15 us
    dot_general x1, matrix products, shards(): jnp.einsum('erf,erd->efd', hidden, grads_full, preferred_element_type=jnp...  8.06 us
  transfers between devices with their start and end apart: 6, of which 4 were waited for; matrix products, arithmetic and copies ran while one was open for 20% of the time, Pallas kernels for 0%

commit v1 on v0

v1 whole, which is shorter than its diff:
```python
import functools

import jax
import jax.numpy as jnp
from jax import lax
from jax.experimental import pallas as pl
from jax.experimental.pallas import tpu as pltpu
from jax.sharding import PartitionSpec as P

MESH = pl.DeviceIdType.MESH
BF = jnp.bfloat16
F32 = jnp.float32


def flip(index, mask, count):
    out = index
    bit = 1
    while bit < count:
        if mask & bit:
            out = out + (1 - 2 * ((index // bit) % 2)) * bit
        bit *= 2
    return out


def dot(a, b, ca=1, cb=0):
    return lax.dot_general(a, b, (((ca,), (cb,)), ((), ())), preferred_element_type=F32)


def kernel(E, cap, L, TILE,
           trow, tcol, tok, grd, wi_h, wo_h,
           mix_o, gin_o, gwi_o, gwo_o,
           sib_t, sib_g, send_t, send_g, xb, gb, wi, wo, gwi, gwo, hid, gh,
           part, gpart, cb, gcb, ys, gys, yr, gyr, fin, gfin, back, gback,
           tp, gtp, rtp, rgtp, ssem, rsem, lsem):
    Lh = L // 2
    R = Lh * cap
    F = tok.shape[1]
    D = 2 * F
    rows = E * cap
    FS = wi.shape[2]
    T = tok.shape[0]
    e = lax.axis_index("expert")
    s = lax.axis_index("slab")
    h = s // 2
    c = s % 2
    sib = (e, 2 * h + 1 - c)
    ym = (e, 2 * (1 - h) + c)

    load_wi = pltpu.make_async_copy(wi_h, wi, lsem.at[0])
    load_wo = pltpu.make_async_copy(wo_h, wo, lsem.at[1])
    load_wi.start()
    load_wo.start()

    barrier = pltpu.get_barrier_semaphore()
    peers = [sib, ym] + [(flip(e, k, E), s) for k in range(1, E)]
    for p in peers:
        pl.semaphore_signal(barrier, inc=1, device_id=p, device_id_type=MESH)
    pl.semaphore_wait(barrier, len(peers))

    started = []

    def send(src, dst, dev):
        n = len(started)
        copy = pltpu.make_async_remote_copy(
            src_ref=src, dst_ref=dst, send_sem=ssem.at[n], recv_sem=rsem.at[n],
            device_id=dev, device_id_type=MESH)
        copy.start()
        started.append(copy)
        return copy

    order = list(range(E - 1, 0, -1))
    mine = pl.ds(c * Lh, Lh)

    c_t = send(tok, sib_t, sib)
    c_g = send(grd, sib_g, sib)

    def scatter(copy, own, other, stage, buf):
        copy.wait_recv()
        other[...] = own[...] + other[...]
        a2a = {}
        for k in order + [0]:
            dest = flip(e, k, E)
            row = lax.broadcasted_iota(jnp.int32, (R, T), 0) + dest * R
            place = jnp.where(row == trow[...], 1.0, 0.0).astype(BF)
            val = dot(place, other[...]).astype(BF).reshape(Lh, cap, F)
            if k == 0:
                buf[h, mine, e] = val
            else:
                stage[k] = val
                a2a[k] = send(stage.at[k], buf.at[h, mine, e], (dest, s))
        return a2a

    ycopy = {}
    waits = {"t": [], "g": []}

    def pass_on(tag, buf, a2a, k):
        if k:
            a2a[k].wait_recv()
        ref = buf.at[h, mine, flip(e, k, E)]
        ycopy[tag, k] = send(ref, ref, ym)
        waits[tag].append(send(ref, ref, sib))

    def pass_y(tag, buf, k):
        ycopy[tag, k].wait_recv()
        ref = buf.at[1 - h, mine, flip(e, k, E)]
        waits[tag].append(send(ref, ref, sib))

    a2a_t = scatter(c_t, tok, sib_t, send_t, xb)
    pass_on("t", xb, a2a_t, 0)
    a2a_g = scatter(c_g, grd, sib_g, send_g, gb)
    arrive = [0] + order[::-1]
    for i, k in enumerate(arrive):
        if k:
            pass_on("t", xb, a2a_t, k)
        if i >= 2:
            pass_y("t", xb, arrive[i - 2])
    for k in arrive[-2:]:
        pass_y("t", xb, k)
    for w in waits["t"]:
        w.wait_recv()
    load_wi.wait()
    load_wo.wait()

    def whole(buf, l):
        return jnp.concatenate(
            [buf[0, l].reshape(rows, F), buf[1, l].reshape(rows, F)], axis=1)

    def tile(n):
        return pl.ds(pl.multiple_of(n * TILE, TILE), TILE)

    def forward(l):
        @pl.loop(0, FS // TILE)
        def _(n):
            pre = dot(whole(xb, l), wi[l, :, tile(n)])
            hid[l, :, tile(n)] = jnp.maximum(pre, 0.0).astype(BF)

        @pl.loop(0, D // TILE)
        def _(n):
            part[l, :, tile(n)] = dot(hid[l], wo[l, :, tile(n)]).astype(BF)

    def backward(l):
        @pl.loop(0, FS // TILE)
        def _(n):
            g = dot(whole(gb, l), wo[l, tile(n), :], 1, 1)
            gh[l, :, tile(n)] = jnp.where(
                hid[l, :, tile(n)].astype(F32) > 0.0, g, 0.0).astype(BF)

        @pl.loop(0, D // TILE)
        def _(n):
            gpart[l, :, tile(n)] = dot(gh[l], wi[l, tile(n), :], 1, 1).astype(BF)

    stores = []

    def weights(l):
        @pl.loop(0, FS // TILE)
        def _(n):
            gwo[l, tile(n), :] = dot(hid[l, :, tile(n)], whole(gb, l), 0, 0).astype(BF)

        put = pltpu.make_async_copy(gwo.at[l], gwo_o.at[l], lsem.at[2 + 2 * l])
        put.start()
        stores.append(put)

        @pl.loop(0, 2)
        def _(n):
            gwi[l, pl.ds(pl.multiple_of(n * F, F), F), :] = dot(
                xb[n, l].reshape(rows, F), gh[l], 0, 0).astype(BF)

        put = pltpu.make_async_copy(gwi.at[l], gwi_o.at[l], lsem.at[3 + 2 * l])
        put.start()
        stores.append(put)

    def half(which):
        return pl.ds(pl.multiple_of(which * F, 128), F)

    def combine(copy, own, other, stage, land, j):
        copy.wait_recv()
        l = c * Lh + j
        stage[j] = (own[l, :, half(1 - h)].astype(F32)
                    + other[j, :, half(1 - h)].astype(F32)).astype(BF)
        return send(stage.at[j], land.at[j], ym)

    def finish(copy, own, other, land, final, out, j):
        copy.wait_recv()
        l = c * Lh + j
        total = (own[l, :, half(h)].astype(F32) + other[j, :, half(h)].astype(F32)
                 + land[j].astype(F32)).astype(BF)
        final[j] = total.reshape(E, cap, F)
        res = []
        for k in order:
            dest = flip(e, k, E)
            res.append(send(final.at[j, dest], out.at[e, j], (dest, s)))
        out[e, j] = final[j, e]
        return res

    share = -(-E // L)
    csend = []
    for j in range(Lh):
        l = (1 - c) * Lh + j
        forward(l)
        csend.append(send(part.at[l], cb.at[j], sib))
        for k in arrive[j * share:(j + 1) * share]:
            pass_on("g", gb, a2a_g, k)
    for j in range(Lh, L):
        forward(c * Lh + j - Lh)
        for k in arrive[j * share:(j + 1) * share]:
            pass_on("g", gb, a2a_g, k)
    ysend = [combine(csend[j], part, cb, ys, yr, j) for j in range(Lh)]
    for k in arrive:
        pass_y("g", gb, k)
    for w in waits["g"]:
        w.wait_recv()

    gcsend, bsend, gbsend = [], [], []
    for j in range(Lh):
        l = (1 - c) * Lh + j
        backward(l)
        gcsend.append(send(gpart.at[l], gcb.at[j], sib))
    gysend = []
    for j in range(Lh):
        backward(c * Lh + j)
        gysend.append(combine(gcsend[j], gpart, gcb, gys, gyr, j))
        bsend += finish(ysend[j], part, cb, yr, fin, back, j)
    for l in range(L):
        weights(l)
        if l % 2:
            gbsend += finish(gysend[l // 2], gpart, gcb, gyr, gfin, gback, l // 2)

    def collect(copies, out, stage, land):
        for w in copies:
            w.wait_recv()

        @pl.loop(0, T // 256)
        def _(n):
            at = pl.ds(pl.multiple_of(n * 256, 256), 256)
            row = lax.broadcasted_iota(jnp.int32, (256, E * R), 1)
            pick = jnp.where(row == tcol[at, :], 1.0, 0.0).astype(BF)
            stage[at, :] = dot(pick, out[...].reshape(E * R, F)).astype(BF)

        return send(stage, land, sib)

    last = collect(bsend, back, tp, rtp)
    glast = collect(gbsend, gback, gtp, rgtp)
    last.wait_recv()
    mix_o[...] = tp[...] + rtp[...]
    glast.wait_recv()
    gin_o[...] = gtp[...] + rgtp[...]
    for copy in started:
        copy.wait_send()
    for put in stores:
        put.wait()


def shards(tokens, gate, routes, grad_out, w_in, w_out):
    T, Q = tokens.shape
    E = lax.axis_size("expert")
    L, D, FS = w_in.shape
    X = E * L
    cap = 2 * T // X
    Lh = L // 2
    F = 2 * Q
    c = lax.axis_index("slab") % 2
    ids = routes[:, 0]
    onehot = ids[:, None] == jnp.arange(X, dtype=jnp.int32)[None, :]
    at = jnp.arange(T, dtype=jnp.int32)
    before = (at[:, None] > at[None, :]).astype(BF)
    earlier = jnp.dot(before, onehot.astype(BF), preferred_element_type=F32)
    slot = jnp.sum(jnp.where(onehot, earlier, 0.0), axis=1).astype(jnp.int32)
    local = ids % L
    target = jnp.where(
        local // Lh == c, (ids // L) * (Lh * cap) + (local % Lh) * cap + slot, -1)
    scaled = (gate[:, None] * grad_out.astype(F32)).astype(BF)

    def widen(v):
        z = jnp.zeros_like(v)
        return jnp.where(c == 0, jnp.concatenate([v, z], 1), jnp.concatenate([z, v], 1))

    rows = E * cap
    TILE = 256
    n_sem = 2 * (6 * E + 3)
    vm = lambda shape, t=BF: pltpu.VMEM(shape, t)
    two = lambda shape: [vm(shape), vm(shape)]
    scratch = (
        two((T, F)) + two((E, Lh, cap, F)) + two((2, L, E, cap, F))
        + two((L, D, FS)) + [vm((L, D, FS)), vm((L, FS, D))]
        + two((L, rows, FS)) + two((L, rows, D)) + two((Lh, rows, D))
        + two((Lh, rows, F)) + two((Lh, rows, F)) + two((Lh, E, cap, F))
        + two((E, Lh, cap, F)) + two((T, F)) + two((T, F))
        + [pltpu.SemaphoreType.DMA((n_sem,)), pltpu.SemaphoreType.DMA((n_sem,)),
           pltpu.SemaphoreType.DMA((2 + 2 * L,))])
    V = pl.BlockSpec(memory_space=pltpu.VMEM)
    A = pl.BlockSpec(memory_space=pl.ANY)
    mix, gin, gwi, gwo = pl.pallas_call(
        functools.partial(kernel, E, cap, L, TILE),
        out_shape=(
            jax.ShapeDtypeStruct((T, F), BF), jax.ShapeDtypeStruct((T, F), BF),
            jax.ShapeDtypeStruct(w_in.shape, BF), jax.ShapeDtypeStruct(w_out.shape, BF)),
        in_specs=[V, V, V, V, A, A],
        out_specs=(V, V, A, A),
        scratch_shapes=scratch,
        compiler_params=pltpu.CompilerParams(
            collective_id=0, has_side_effects=True, vmem_limit_bytes=63 * 2**20),
        cost_estimate=pl.CostEstimate(
            flops=12 * L * rows * D * FS, bytes_accessed=8 * L * D * FS, transcendentals=0),
    )(target[None, :], target[:, None], widen(tokens), widen(scaled), w_in, w_out)
    mix = lax.dynamic_slice(mix, (0, c * Q), (T, Q))
    gin = lax.dynamic_slice(gin, (0, c * Q), (T, Q))
    mixed = (gate[:, None] * mix.astype(F32)).astype(BF)
    return (mixed, gin, gwi, gwo)


def solution(mesh):
    in_specs = (
        P("expert", "slab"),
        P("expert"),
        P("expert", None),
        P("expert", "slab"),
        P("expert", None, "slab"),
        P("expert", "slab", None),
    )
    out_specs = (
        P("expert", "slab"),
        P("expert", "slab"),
        P("expert", None, "slab"),
        P("expert", "slab", None),
    )
    return jax.shard_map(shards, mesh=mesh, in_specs=in_specs, out_specs=out_specs, check_vma=False)
```

time: 242 us -> 141 us (0.58)
  Pallas kernels: 0 us -> 116 us
  waiting for transfers between devices: 84.9 us -> 0 us
  blocking collectives: 60 us -> 0 us
  matrix products: 45.7 us -> 1.3 us
  between operations: 14 us -> 0.74 us
  starting transfers between devices: 10.8 us -> 0 us
  other arithmetic: 11.3 us -> 7.97 us
    pallas_call x0 -> x1, Pallas kernels: none -> 116 us  [shards(): pl.pallas_call(functools.partial(kernel, E, cap, L, TILE), out_shape=(jax...]
    reduce_scatter x2 -> x0, waiting for transfers between devices: 62.1 us -> none  [the longest x1 33.6 us: shards(): lax.psum_scatter(grad_part, 'slab', scatter_dimension=2, tiled=True)]
    all_to_all x2 -> x0, blocking collectives: 60 us -> none  [the longest x1 31.2 us: shards(): lax.all_to_all(rows_send, 'expert', split_axis=0, concat_axis=1, tiled=True)]
    dot_general x10 -> x1, matrix products: 45.7 us -> 1.3 us  [shards(): earlier = jnp.dot(before, onehot.astype(BF), preferred_element_type=F32)]
    all_gather x2 -> x0, waiting for transfers between devices: 13.2 us -> none  [the longest x1 13.2 us: shards(): grads_full = lax.all_gather(grads_recv, 'slab', axis=2, tiled=True)]
    all_to_all x2 -> x0, starting transfers between devices: 10.5 us -> none  [the longest x1 5.23 us: shards(): lax.all_to_all(grad_sum.astype(jnp.bfloat16), 'expert', split_axis=1, con...]
    all_to_all x2 -> x0, waiting for transfers between devices: 9.57 us -> none  [the longest x1 9.57 us: shards(): lax.all_to_all(grad_sum.astype(jnp.bfloat16), 'expert', split_axis=1, con...]
    another operation x3 -> x0, other arithmetic: 9.15 us -> none
  transfers between devices with their start and end apart: 6 -> 0, of which waited for: 4 -> 0; matrix products, arithmetic and copies ran while one was open for 20% -> 0% of each run, Pallas kernels for 0% -> 0%
where the time goes in v1:
time: 141 us; the launch traced here: 140 us
  Pallas kernels  116 us (82%)
  local copies, waits for them, and re-layouts  13.5 us (10%)
  other arithmetic  7.97 us (6%)
    pallas_call x1, Pallas kernels, shards(): pl.pallas_call(functools.partial(kernel, E, cap, L, TILE), out_shape=(jax...  116 us
    unnamed x15, local copies, waits for them, and re-layouts  11.7 us
    select_n x2, other arithmetic, shards(): jnp.where(local // Lh == c, ids // L * (Lh * cap) + local % Lh * cap + sl...  3.17 us

profile of v1, /device:TPU:1, one launch (start us, length us, event | category | flops | bytes accessed | tf_op | source)
XLA Modules:
  0.0 139.9 jit_solution(7749458349505374741)
XLA Ops:
  0.6 0.0 copy-start
  0.7 1.3 fusion.2
  2.0 1.4 compare_select_fusion.trow
  3.3 0.7 broadcast_compare_fusion
  4.0 0.3 copy.26
  4.3 0.2 copy.29
  4.6 1.2 copy.30
  5.8 1.2 copy.32
  7.0 0.9 multiply_convert_fusion.1
  7.9 1.8 %pad_select_fusion = (bf16[1024,384]{1,0:T(8,128)(2,1)}, bf16[1024,384]{1,0:T(8,128)(2,1)}) fusion(bf16[1024,192]{1,0:T(8,128)(2,1)S(1)} %multiply_convert_fusion.1, pred[]{:T(512)S(6)} %eq.50, bf16[1024,192]{1,0:T(8,128)(2,1)S(1)} %copy.30), kind=kLoop, calls=%fused_computation.6 | loop fusion | flops 786432 | bytes 2359297 | tf_op jit(solution)/shard_map/jit(_where)/select_n | solution.py:275
  9.6 0.0 copy-done
  9.6 0.2 copy.23
  9.9 1.8 %fusion.7.tcol = s32[1024,1]{1,0:T(8,128)} fusion(s32[1024,1]{1,0:T(8,128)S(1)} %copy.29, pred[1024,1]{1,0:T(8,128)(4,1)S(1)} %copy.26, s32[1024,1]{1,0:T(8,128)S(1)} %copy.23, s32[]{:T(128)S(6)} %select_n.101), kind=kLoop, calls=%fused_computation.22 | loop fusion | flops 44032 | bytes 13316 | tf_op jit(solution)/shard_map/jit(_where)/select_n | solution.py:269
  11.7 0.0 copy-start.1
  11.7 116.4 %shard_map.93 = (bf16[1024,384]{1,0:T(8,128)(2,1)}, bf16[1024,384]{1,0:T(8,128)(2,1)}, bf16[4,768,768]{2,1,0:T(8,128)(2,1)}, bf16[4,768,768]{2,1,0:T(8,128)(2,1)}) custom-call(s32[1,1024]{1,0:T(1,128)} %compare_select_fusion.trow, s32[1024,1]{1,0:T(8,128)} %fusion.7.tcol, bf16[1024,384]{1,0:T(8,128)(2,1)} %get-tuple-element.21.tok, ...), custom_call_target="tpu_custom_call" | custom-call | flops 14495514624 | bytes 18874368 | tf_op jit(solution)/shard_map/pallas_call | solution.py:292
  128.1 0.0 copy-done.1
  128.1 1.4 %multiply_convert_fusion = bf16[1024,192]{1,0:T(8,128)(2,1)S(1)} fusion(bf16[1024,384]{1,0:T(8,128)(2,1)} %get-tuple-element.8, s32[]{:T(128)S(6)} %select_n.114, f32[1024]{0:T(1024)S(1)} %copy-done.1), kind=kLoop, calls=%fused_computation.4 | loop fusion | flops 589824 | bytes 790532 | tf_op jit(solution)/shard_map/convert_element_type | solution.py:307
  129.6 1.3 constant_dynamic-slice_fusion
  130.8 0.9 copy.34
  131.8 0.0 slice-start
  131.8 0.9 copy.33
  132.7 0.0 slice-start.1
  132.7 5.0 %copy.44 = bf16[4,768,768]{2,1,0:T(8,128)(2,1)} copy(bf16[4,768,768]{2,1,0:T(8,128)(2,1)} %get-tuple-element.28) | data formatting | bytes 9437184
  137.7 0.0 slice-done
  137.7 0.0 slice-done.1
  137.7 2.2 %copy.45 = bf16[4,768,768]{2,1,0:T(8,128)(2,1)} copy(bf16[4,768,768]{2,1,0:T(8,128)(2,1)S(1)} %bitcast.19) | data formatting | bytes 9437184
  (2 shorter events, 0.0 us)
Async XLA Ops:
  0.6 9.0 %copy-start = (s32[1024,1]{0,1:T(1,128)S(1)}, s32[1024,1]{0,1:T(1,128)}, u32[]{:S(2)}) copy-start(s32[1024,1]{0,1:T(1,128)} %param.8) | copy-start | bytes 12292
  11.7 116.4 %copy-start.1 = (f32[1024]{0:T(1024)S(1)}, f32[1024]{0:T(1024)}, u32[]{:S(2)}) copy-start(f32[1024]{0:T(1024)} %param.7) | copy-start | bytes 12292
  131.8 5.9 %slice-start = ((s8[4718592]{0:T(1024)(128)(4,1)}), s8[524288]{0:T(1024)(128)(4,1)S(1)}, s32[]{:S(2)}) async-start(s8[4718592]{0:T(1024)(128)(4,1)} %bitcast.18), calls=%async_computation | async-start | bytes 1048576
  132.7 5.0 %slice-start.1 = ((s8[4718592]{0:T(1024)(128)(4,1)}), s8[4194304]{0:T(1024)(128)(4,1)S(1)}, s32[]{:S(2)}) async-start(s8[4718592]{0:T(1024)(128)(4,1)} %bitcast.18), calls=%async_computation.1 | async-start | bytes 8388608

commit v2 on v1

v2 whole, which is shorter than its diff:
```python
import functools

import jax
import jax.numpy as jnp
from jax import lax
from jax.experimental import pallas as pl
from jax.experimental.pallas import tpu as pltpu
from jax.sharding import PartitionSpec as P

MESH = pl.DeviceIdType.MESH
BF = jnp.bfloat16
F32 = jnp.float32


def flip(index, mask, count):
    out = index
    bit = 1
    while bit < count:
        if mask & bit:
            out = out + (1 - 2 * ((index // bit) % 2)) * bit
        bit *= 2
    return out


def dot(a, b, ca=1, cb=0):
    return lax.dot_general(a, b, (((ca,), (cb,)), ((), ())), preferred_element_type=F32)


def kernel(E, cap, L, TILE,
           routes, gate, tok, grd, wi_h, wo_h,
           mix_o, gin_o, gwi_o, gwo_o,
           trow, cat_t, cat_g, send_t, send_g, xb, gb, wi, wo, gwi, gwo, hid, gh,
           part, gpart, cb, gcb, ys, gys, yr, gyr, fin, gfin, back, gback,
           tp, gtp, rtp, rgtp, ssem, rsem, lsem):
    Lh = L // 2
    R = Lh * cap
    Q, T = tok.shape
    F = 2 * Q
    D = 2 * F
    X = E * L
    rows = E * cap
    FS = wi.shape[2]
    e = lax.axis_index("expert")
    s = lax.axis_index("slab")
    h = s // 2
    c = s % 2
    sib = (e, 2 * h + 1 - c)
    ym = (e, 2 * (1 - h) + c)

    load_wi = pltpu.make_async_copy(wi_h, wi, lsem.at[0])
    load_wo = pltpu.make_async_copy(wo_h, wo, lsem.at[1])
    load_wi.start()
    load_wo.start()

    barrier = pltpu.get_barrier_semaphore()
    peers = [sib, ym] + [(flip(e, k, E), s) for k in range(1, E)]
    for p in peers:
        pl.semaphore_signal(barrier, inc=1, device_id=p, device_id_type=MESH)

    ids = routes[...]
    onehot = (lax.broadcasted_iota(jnp.int32, (X, T), 0) == ids).astype(F32)
    STEP = 256
    for n in range(T // STEP):
        at = slice(n * STEP, (n + 1) * STEP)
        before = (lax.broadcasted_iota(jnp.int32, (T, STEP), 0)
                  < lax.broadcasted_iota(jnp.int32, (T, STEP), 1) + n * STEP)
        earlier = dot(onehot.astype(BF), jnp.where(before, 1.0, 0.0).astype(BF))
        slot = jnp.sum(earlier * onehot[:, at], axis=0, keepdims=True).astype(jnp.int32)
        local = lax.rem(ids[:, at], L)
        trow[:, at] = jnp.where(
            lax.div(local, Lh) == c,
            lax.div(ids[:, at], L) * R + lax.rem(local, Lh) * cap + slot, -1)
    cat_g[c] = (gate[...] * grd[...].astype(F32)).astype(BF)
    cat_t[c] = tok[...]
    pl.semaphore_wait(barrier, len(peers))

    started = []

    def send(src, dst, dev):
        n = len(started)
        copy = pltpu.make_async_remote_copy(
            src_ref=src, dst_ref=dst, send_sem=ssem.at[n], recv_sem=rsem.at[n],
            device_id=dev, device_id_type=MESH)
        copy.start()
        started.append(copy)
        return copy

    far, near = list(range(E // 2, E)), list(range(1, E // 2))
    order = [k for i, f in enumerate(far) for k in ([f] + near[i:i + 1])]
    mine = pl.ds(c * Lh, Lh)

    c_t = send(cat_t.at[c], cat_t.at[c], sib)
    c_g = send(cat_g.at[c], cat_g.at[c], sib)

    def scatter(k, cat, stage, buf):
        dest = flip(e, k, E)
        row = lax.broadcasted_iota(jnp.int32, (R, T), 0) + dest * R
        place = jnp.where(row == trow[...], 1.0, 0.0).astype(BF)
        val = dot(place, cat[...].reshape(F, T), 1, 1).astype(BF).reshape(Lh, cap, F)
        if k == 0:
            buf[h, mine, e] = val
            return None
        stage[k] = val
        return send(stage.at[k], buf.at[h, mine, e], (dest, s))

    ycopy = {}
    waits = {"t": [], "g": []}

    def pass_on(tag, buf, a2a, k):
        if k:
            a2a[k].wait_recv()
        ref = buf.at[h, mine, flip(e, k, E)]
        ycopy[tag, k] = send(ref, ref, ym)
        waits[tag].append(send(ref, ref, sib))

    def pass_y(tag, buf, k):
        ycopy[tag, k].wait_recv()
        ref = buf.at[1 - h, mine, flip(e, k, E)]
        waits[tag].append(send(ref, ref, sib))

    arrive = [0] + order
    c_t.wait_recv()
    a2a_t = {k: scatter(k, cat_t, send_t, xb) for k in order + [0]}
    c_g.wait_recv()
    a2a_g = {}
    for i, k in enumerate(arrive):
        pass_on("t", xb, a2a_t, k)
        g = arrive[(i + 1) % E]
        a2a_g[g] = scatter(g, cat_g, send_g, gb)
        if i >= 2:
            pass_y("t", xb, arrive[i - 2])
    for k in arrive[-2:]:
        pass_y("t", xb, k)
    for w in waits["t"]:
        w.wait_recv()
    load_wi.wait()
    load_wo.wait()

    def whole(buf, l):
        return jnp.concatenate(
            [buf[0, l].reshape(rows, F), buf[1, l].reshape(rows, F)], axis=1)

    def tile(n):
        return pl.ds(pl.multiple_of(n * TILE, TILE), TILE)

    def forward(l):
        @pl.loop(0, FS // TILE)
        def _(n):
            pre = dot(whole(xb, l), wi[l, :, tile(n)])
            hid[l, :, tile(n)] = jnp.maximum(pre, 0.0).astype(BF)

        @pl.loop(0, D // TILE)
        def _(n):
            part[l, :, tile(n)] = dot(hid[l], wo[l, :, tile(n)]).astype(BF)

    def backward(l):
        @pl.loop(0, FS // TILE)
        def _(n):
            g = dot(whole(gb, l), wo[l, tile(n), :], 1, 1)
            gh[l, :, tile(n)] = jnp.where(
                hid[l, :, tile(n)].astype(F32) > 0.0, g, 0.0).astype(BF)

        @pl.loop(0, D // TILE)
        def _(n):
            gpart[l, :, tile(n)] = dot(gh[l], wi[l, tile(n), :], 1, 1).astype(BF)

    stores = []

    def weights(l):
        @pl.loop(0, FS // TILE)
        def _(n):
            gwo[l, tile(n), :] = dot(hid[l, :, tile(n)], whole(gb, l), 0, 0).astype(BF)

        put = pltpu.make_async_copy(gwo.at[l], gwo_o.at[l], lsem.at[2 + 2 * l])
        put.start()
        stores.append(put)

        @pl.loop(0, 2)
        def _(n):
            gwi[l, pl.ds(pl.multiple_of(n * F, F), F), :] = dot(
                xb[n, l].reshape(rows, F), gh[l], 0, 0).astype(BF)

        put = pltpu.make_async_copy(gwi.at[l], gwi_o.at[l], lsem.at[3 + 2 * l])
        put.start()
        stores.append(put)

    def half(which):
        return pl.ds(pl.multiple_of(which * F, 128), F)

    def group(p):
        top = e // (E // 2)
        return (1 - top if p == 0 else top) * (E // 2)

    def combine(own, other, stage, land, j, p):
        l = c * Lh + j
        g = group(p)
        at = pl.ds(pl.multiple_of(g * cap, cap), E // 2 * cap)
        stage[j, at, :] = (own[l, at, half(1 - h)].astype(F32)
                           + other[j, at, half(1 - h)].astype(F32)).astype(BF)
        return send(stage.at[j, at], land.at[j, at], ym)

    def finish(copy, own, other, land, final, out, j, p):
        copy.wait_recv()
        l = c * Lh + j
        g = group(p)
        at = pl.ds(pl.multiple_of(g * cap, cap), E // 2 * cap)
        total = (own[l, at, half(h)].astype(F32) + other[j, at, half(h)].astype(F32)
                 + land[j, at, :].astype(F32)).astype(BF)
        final[j, pl.ds(g, E // 2)] = total.reshape(E // 2, cap, F)
        res = []
        for k in order:
            if (k >= E // 2) == (p == 0):
                dest = flip(e, k, E)
                res.append(send(final.at[j, dest], out.at[e, j], (dest, s)))
        if p == 1:
            out[e, j] = final[j, e]
        return res

    share = -(-E // L)
    csend = []
    for j in range(Lh):
        l = (1 - c) * Lh + j
        forward(l)
        csend.append(send(part.at[l], cb.at[j], sib))
        for k in arrive[j * share:(j + 1) * share]:
            pass_on("g", gb, a2a_g, k)
    for j in range(Lh, L):
        forward(c * Lh + j - Lh)
        for k in arrive[j * share:(j + 1) * share]:
            pass_on("g", gb, a2a_g, k)
    ysend, gysend = {}, {}
    for j in range(Lh):
        csend[j].wait_recv()
        for p in range(2):
            ysend[j, p] = combine(part, cb, ys, yr, j, p)
    for k in arrive:
        pass_y("g", gb, k)
    for w in waits["g"]:
        w.wait_recv()

    steps = [(j, p) for j in range(Lh) for p in range(2)]
    gcsend, bsend, gbsend = [], [], []
    for i in range(L):
        j = i % Lh
        l = (1 - c) * Lh + j if i < Lh else c * Lh + j
        backward(l)
        if i < Lh:
            gcsend.append(send(gpart.at[l], gcb.at[j], sib))
        else:
            gcsend[j].wait_recv()
            for p in range(2):
                gysend[j, p] = combine(gpart, gcb, gys, gyr, j, p)
        for st in steps[i * 2 * Lh // L:(i + 1) * 2 * Lh // L]:
            bsend += finish(ysend[st], part, cb, yr, fin, back, *st)

    def collect(copies, out, stage, land):
        for w in copies:
            w.wait_recv()
        for n in range(T // 512):
            at = slice(n * 512, (n + 1) * 512)
            row = lax.broadcasted_iota(jnp.int32, (E * R, 512), 0)
            pick = jnp.where(row == trow[:, at], 1.0, 0.0).astype(BF)
            val = dot(out[...].reshape(E * R, F), pick, 0, 0).astype(BF)
            stage[0, :, at] = val[:Q]
            stage[1, :, at] = val[Q:]
        return send(stage.at[1 - c], land, sib)

    for i in range(L):
        weights(i)
        for st in steps[i * 2 * Lh // L:(i + 1) * 2 * Lh // L]:
            gbsend += finish(gysend[st], gpart, gcb, gyr, gfin, gback, *st)
    last = collect(bsend, back, tp, rtp)
    last.wait_recv()
    mix_o[...] = (gate[...] * (tp[c].astype(F32) + rtp[...].astype(F32))).astype(BF)
    glast = collect(gbsend, gback, gtp, rgtp)
    glast.wait_recv()
    gin_o[...] = gtp[c] + rgtp[...]
    for copy in started:
        copy.wait_send()
    for put in stores:
        put.wait()


def shards(tokens, gate, routes, grad_out, w_in, w_out):
    T, Q = tokens.shape
    E = lax.axis_size("expert")
    L, D, FS = w_in.shape
    X = E * L
    cap = 2 * T // X
    Lh = L // 2
    F = 2 * Q
    rows = E * cap
    TILE = 256
    n_sem = 2 * (6 * E + 5)
    vm = lambda shape, t=BF: pltpu.VMEM(shape, t)
    two = lambda shape: [vm(shape), vm(shape)]
    scratch = (
        [vm((1, T), jnp.int32)] + two((2, Q, T)) + two((E, Lh, cap, F)) + two((2, L, E, cap, F))
        + two((L, D, FS)) + [vm((L, D, FS)), vm((L, FS, D))]
        + two((L, rows, FS)) + two((L, rows, D)) + two((Lh, rows, D))
        + two((Lh, rows, F)) + two((Lh, rows, F)) + two((Lh, E, cap, F))
        + two((E, Lh, cap, F)) + two((2, Q, T)) + two((Q, T))
        + [pltpu.SemaphoreType.DMA((n_sem,)), pltpu.SemaphoreType.DMA((n_sem,)),
           pltpu.SemaphoreType.DMA((2 + 2 * L,))])
    V = pl.BlockSpec(memory_space=pltpu.VMEM)
    A = pl.BlockSpec(memory_space=pl.ANY)
    mix, gin, gwi, gwo = pl.pallas_call(
        functools.partial(kernel, E, cap, L, TILE),
        out_shape=(
            jax.ShapeDtypeStruct((Q, T), BF), jax.ShapeDtypeStruct((Q, T), BF),
            jax.ShapeDtypeStruct(w_in.shape, BF), jax.ShapeDtypeStruct(w_out.shape, BF)),
        in_specs=[V, V, V, V, A, A],
        out_specs=(V, V, A, A),
        scratch_shapes=scratch,
        compiler_params=pltpu.CompilerParams(
            collective_id=0, has_side_effects=True, vmem_limit_bytes=63 * 2**20),
        cost_estimate=pl.CostEstimate(
            flops=12 * L * rows * D * FS, bytes_accessed=8 * L * D * FS, transcendentals=0),
    )(routes.reshape(1, T), gate[None, :], tokens.T, grad_out.T, w_in, w_out)
    return (mix.T, gin.T, gwi, gwo)


def solution(mesh):
    in_specs = (
        P("expert", "slab"),
        P("expert"),
        P("expert", None),
        P("expert", "slab"),
        P("expert", None, "slab"),
        P("expert", "slab", None),
    )
    out_specs = (
        P("expert", "slab"),
        P("expert", "slab"),
        P("expert", None, "slab"),
        P("expert", "slab", None),
    )
    return jax.shard_map(shards, mesh=mesh, in_specs=in_specs, out_specs=out_specs, check_vma=False)
```

time: 141 us -> 116 us (0.82)
  Pallas kernels: 116 us -> 104 us
  other arithmetic: 7.97 us -> 0.01 us
  local copies, waits for them, and re-layouts: 13.5 us -> 10.8 us
    pallas_call x1, Pallas kernels: 116 us -> 104 us  [shards(): pl.pallas_call(functools.partial(kernel, E, cap, L, TILE), out_shape=(jax...]
    select_n x3 -> x0, other arithmetic: 4.94 us -> none  [the longest x2 3.17 us: shards(): jnp.where(local // Lh == c, ids // L * (Lh * cap) + local % Lh * cap + sl...]
    convert_element_type x3 -> x0, other arithmetic: 2.33 us -> none  [the longest x1 1.44 us: shards(): mixed = (gate[:, None] * mix.astype(F32)).astype(BF)]
    unnamed x15 -> x8, local copies, waits for them, and re-layouts: 11.7 us -> 10.8 us
where the time goes in v2:
time: 116 us
  Pallas kernels  104 us (90%)
  local copies, waits for them, and re-layouts  10.8 us (9%)
    pallas_call x1, Pallas kernels, shards(): pl.pallas_call(functools.partial(kernel, E, cap, L, TILE), out_shape=(jax...  104 us
    unnamed x8, local copies, waits for them, and re-layouts  10.8 us

profile of v2, /device:TPU:1, one launch (start us, length us, event | category | flops | bytes accessed | tf_op | source)
XLA Modules:
  0.0 115.9 jit_solution(13150971032412585129)
XLA Ops:
  0.6 104.5 %shard_map.93 = (bf16[192,1024]{1,0:T(8,128)(2,1)}, bf16[192,1024]{1,0:T(8,128)(2,1)}, bf16[4,768,768]{2,1,0:T(8,128)(2,1)}, bf16[4,768,768]{2,1,0:T(8,128)(2,1)}) custom-call(s32[1,1024]{1,0:T(1,128)} %bitcast.12, f32[1,1024]{1,0:T(1,128)} %bitcast.13, bf16[192,1024]{1,0:T(8,128)(2,1)} %bitcast.10, bf16[192,1024]{1,0:T(8,128)(2,1)} %bitcast.11, ...), custom_call_target="tpu_custom_call" | custom-call | flops 14495514624 | bytes 18874368 | tf_op jit(solution)/shard_map/pallas_call | solution.py:307
  105.1 1.8 %copy.14 = bf16[1024,192]{0,1:T(8,128)(2,1)} copy(bf16[1024,192]{0,1:T(8,128)(2,1)} %bitcast.9) | data formatting | bytes 786432
  106.9 0.0 slice-start
  106.9 1.9 %copy.15 = bf16[1024,192]{0,1:T(8,128)(2,1)} copy(bf16[1024,192]{0,1:T(8,128)(2,1)} %bitcast.8) | data formatting | bytes 786432
  108.8 0.0 slice-start.1
  108.8 4.9 %copy.16 = bf16[4,768,768]{2,1,0:T(8,128)(2,1)} copy(bf16[4,768,768]{2,1,0:T(8,128)(2,1)} %get-tuple-element.18) | data formatting | bytes 9437184
  113.7 0.0 slice-done
  113.7 0.0 slice-done.1
  113.7 2.2 %copy.17 = bf16[4,768,768]{2,1,0:T(8,128)(2,1)} copy(bf16[4,768,768]{2,1,0:T(8,128)(2,1)S(1)} %bitcast.7) | data formatting | bytes 9437184
  (1 shorter events, 0.0 us)
Async XLA Ops:
  106.9 6.8 %slice-start = ((s8[4718592]{0:T(1024)(128)(4,1)}), s8[4194304]{0:T(1024)(128)(4,1)S(1)}, s32[]{:S(2)}) async-start(s8[4718592]{0:T(1024)(128)(4,1)} %bitcast.6), calls=%async_computation | async-start | bytes 8388608
  108.8 4.9 %slice-start.1 = ((s8[4718592]{0:T(1024)(128)(4,1)}), s8[524288]{0:T(1024)(128)(4,1)S(1)}, s32[]{:S(2)}) async-start(s8[4718592]{0:T(1024)(128)(4,1)} %bitcast.6), calls=%async_computation.1 | async-start | bytes 1048576

commit v3 on v2

--- a/solution.py
+++ b/solution.py
@@ -129,8 +129,11 @@
         a2a_g[g] = scatter(g, cat_g, send_g, gb)
         if i >= 2:
             pass_y("t", xb, arrive[i - 2])
-    for k in arrive[-2:]:
+    early, rest = arrive[:3], arrive[3:]
+    pass_on("g", gb, a2a_g, early[0])
+    for i, k in enumerate(arrive[-2:]):
         pass_y("t", xb, k)
+        pass_on("g", gb, a2a_g, early[1 + i])
     for w in waits["t"]:
         w.wait_recv()
     load_wi.wait()
@@ -216,42 +219,50 @@
             out[e, j] = final[j, e]
         return res
 
-    share = -(-E // L)
+    share = -(-len(rest) // L)
     csend = []
     for j in range(Lh):
         l = (1 - c) * Lh + j
         forward(l)
         csend.append(send(part.at[l], cb.at[j], sib))
-        for k in arrive[j * share:(j + 1) * share]:
+        for k in rest[j * share:(j + 1) * share]:
             pass_on("g", gb, a2a_g, k)
     for j in range(Lh, L):
         forward(c * Lh + j - Lh)
-        for k in arrive[j * share:(j + 1) * share]:
+        for k in rest[j * share:(j + 1) * share]:
             pass_on("g", gb, a2a_g, k)
     ysend, gysend = {}, {}
-    for j in range(Lh):
-        csend[j].wait_recv()
-        for p in range(2):
-            ysend[j, p] = combine(part, cb, ys, yr, j, p)
+    for w in csend:
+        w.wait_recv()
+    steps = [(j, p) for p in range(2) for j in range(Lh)]
+    for st in steps:
+        ysend[st] = combine(part, cb, ys, yr, *st)
     for k in arrive:
         pass_y("g", gb, k)
     for w in waits["g"]:
         w.wait_recv()
 
-    steps = [(j, p) for j in range(Lh) for p in range(2)]
     gcsend, bsend, gbsend = [], [], []
-    for i in range(L):
-        j = i % Lh
-        l = (1 - c) * Lh + j if i < Lh else c * Lh + j
+
+    def out_finish(st):
+        bsend.extend(finish(ysend[st], part, cb, yr, fin, back, *st))
+
+    def grad_finish(st):
+        gbsend.extend(finish(gysend[st], gpart, gcb, gyr, gfin, gback, *st))
+
+    for j in range(Lh):
+        l = (1 - c) * Lh + j
         backward(l)
-        if i < Lh:
-            gcsend.append(send(gpart.at[l], gcb.at[j], sib))
-        else:
-            gcsend[j].wait_recv()
-            for p in range(2):
-                gysend[j, p] = combine(gpart, gcb, gys, gyr, j, p)
-        for st in steps[i * 2 * Lh // L:(i + 1) * 2 * Lh // L]:
-            bsend += finish(ysend[st], part, cb, yr, fin, back, *st)
+        gcsend.append(send(gpart.at[l], gcb.at[j], sib))
+    out_finish(steps[0])
+    for j in range(Lh):
+        backward(c * Lh + j)
+    for w in gcsend:
+        w.wait_recv()
+    for st in steps:
+        gysend[st] = combine(gpart, gcb, gys, gyr, *st)
+    for st in steps[1:]:
+        out_finish(st)
 
     def collect(copies, out, stage, land):
         for w in copies:
@@ -267,9 +278,11 @@
 
     for i in range(L):
         weights(i)
-        for st in steps[i * 2 * Lh // L:(i + 1) * 2 * Lh // L]:
-            gbsend += finish(gysend[st], gpart, gcb, gyr, gfin, gback, *st)
+        if i >= L // 2 - 1:
+            grad_finish(steps[i - L // 2 + 1])
     last = collect(bsend, back, tp, rtp)
+    for st in steps[L - L // 2 + 1:]:
+        grad_finish(st)
     last.wait_recv()
     mix_o[...] = (gate[...] * (tp[c].astype(F32) + rtp[...].astype(F32))).astype(BF)
     glast = collect(gbsend, gback, gtp, rgtp)

time: 116 us -> 114 us (0.983)
    pallas_call x1, Pallas kernels: 104 us -> 103 us  [shards(): pl.pallas_call(functools.partial(kernel, E, cap, L, TILE), out_shape=(jax...]
where the time goes in v3:
time: 114 us
  Pallas kernels  103 us (90%)
  local copies, waits for them, and re-layouts  10.8 us (9%)
    pallas_call x1, Pallas kernels, shards(): pl.pallas_call(functools.partial(kernel, E, cap, L, TILE), out_shape=(jax...  103 us
    unnamed x8, local copies, waits for them, and re-layouts  10.8 us

profile of v3, /device:TPU:1, one launch (start us, length us, event | category | flops | bytes accessed | tf_op | source)
XLA Modules:
  0.0 114.3 jit_solution(9501503638244808278)
XLA Ops:
  0.6 102.9 %shard_map.93 = (bf16[192,1024]{1,0:T(8,128)(2,1)}, bf16[192,1024]{1,0:T(8,128)(2,1)}, bf16[4,768,768]{2,1,0:T(8,128)(2,1)}, bf16[4,768,768]{2,1,0:T(8,128)(2,1)}) custom-call(s32[1,1024]{1,0:T(1,128)} %bitcast.12, f32[1,1024]{1,0:T(1,128)} %bitcast.13, bf16[192,1024]{1,0:T(8,128)(2,1)} %bitcast.10, bf16[192,1024]{1,0:T(8,128)(2,1)} %bitcast.11, ...), custom_call_target="tpu_custom_call" | custom-call | flops 14495514624 | bytes 18874368 | tf_op jit(solution)/shard_map/pallas_call | solution.py:320
  103.5 1.8 %copy.14 = bf16[1024,192]{0,1:T(8,128)(2,1)} copy(bf16[1024,192]{0,1:T(8,128)(2,1)} %bitcast.9) | data formatting | bytes 786432
  105.3 0.0 slice-start
  105.3 1.9 %copy.15 = bf16[1024,192]{0,1:T(8,128)(2,1)} copy(bf16[1024,192]{0,1:T(8,128)(2,1)} %bitcast.8) | data formatting | bytes 786432
  107.2 0.0 slice-start.1
  107.2 4.9 %copy.16 = bf16[4,768,768]{2,1,0:T(8,128)(2,1)} copy(bf16[4,768,768]{2,1,0:T(8,128)(2,1)} %get-tuple-element.18) | data formatting | bytes 9437184
  112.1 0.0 slice-done
  112.1 0.0 slice-done.1
  112.1 2.2 %copy.17 = bf16[4,768,768]{2,1,0:T(8,128)(2,1)} copy(bf16[4,768,768]{2,1,0:T(8,128)(2,1)S(1)} %bitcast.7) | data formatting | bytes 9437184
  (1 shorter events, 0.0 us)
Async XLA Ops:
  105.3 6.8 %slice-start = ((s8[4718592]{0:T(1024)(128)(4,1)}), s8[4194304]{0:T(1024)(128)(4,1)S(1)}, s32[]{:S(2)}) async-start(s8[4718592]{0:T(1024)(128)(4,1)} %bitcast.6), calls=%async_computation | async-start | bytes 8388608
  107.2 4.9 %slice-start.1 = ((s8[4718592]{0:T(1024)(128)(4,1)}), s8[524288]{0:T(1024)(128)(4,1)S(1)}, s32[]{:S(2)}) async-start(s8[4718592]{0:T(1024)(128)(4,1)} %bitcast.6), calls=%async_computation.1 | async-start | bytes 1048576
